TPU v7x, 256 devices: a whole 4x4x8 slice. The times are simulated.
256 devices in a mesh: dp: 4 (over x), ctx: 64 (over y, z, core).
Axes of the slice: x: 4, y: 4, z: 8, core: 2. Of those that a mesh axis runs over, the one named last changes fastest.
Arguments:
- queries: bfloat16 [131072, 1024], P(('dp', 'ctx')), parts along dimension 0, may hold values from -6 to 6
- keys: bfloat16 [131072, 1024], P(('dp', 'ctx')), parts along dimension 0, may hold values from -6 to 6
- values: bfloat16 [131072, 1024], P(('dp', 'ctx')), parts along dimension 0, may hold values from -6 to 6
- clip_ids: int32 [131072], P('dp'), parts along dimension 0, may hold values from 0 to 18, never falling along the last dimension, each value on 1 to 3584 neighbouring positions
Outputs:
- attended: bfloat16 [131072, 1024], P(('dp', 'ctx')), parts along dimension 0
There are 4 independent parts, one for each index of `dp`. A program takes and returns all parts, laid end to end along the dimension named above; each array names one. Nothing has to cross between parts.
Inputs may be any that keep to these rules, and one draw needn't show every extreme that they name: `clip_ids`: clip numbers never fall along the tokens; each clip holds 1 to 3584 tokens and one holds exactly 3584.
All inputs are finite; a program needn't handle non-finite values.
Results may differ from a plain program's by a relative error of at most 0.0059.
Values may be sent and summed in bfloat16 or wider, within the bound.
A program may use at most 128 MiB of HBM per device.

v0:
```python
import math

import jax
import jax.numpy as jnp
from jax import lax
from jax.sharding import PartitionSpec as P

HEAD_DIM = 128
FRAME = 256


def from_behind(x, axis, by):
    size = lax.axis_size(axis)
    pairs = [(i, i + by) for i in range(size) if 0 <= i + by < size]
    return lax.ppermute(x, axis, pairs)


def attend_tile(carry_state, query_heads, query_clip, query_frame, pair_rows, key_start, clip_ids):
    output_acc, running_max, totals = carry_state
    tile_rows = pair_rows.shape[1]
    head_count = query_heads.shape[1]
    head_size = query_heads.shape[2]
    softmax_scale = 1.0 / math.sqrt(head_size)
    key_pos = key_start + jnp.arange(tile_rows, dtype=jnp.int32)
    key_clip = lax.dynamic_slice_in_dim(clip_ids, jnp.maximum(key_start, 0), tile_rows, 0)
    allowed = (
        (key_pos >= 0)[None, :]
        & (key_clip[None, :] == query_clip[:, None])
        & ((key_pos // FRAME)[None, :] <= query_frame[:, None])
    )
    key_heads = pair_rows[0].reshape(tile_rows, head_count, head_size)
    value_heads = pair_rows[1].reshape(tile_rows, head_count, head_size)
    scores = (
        jnp.einsum("qhd,khd->qhk", query_heads, key_heads, preferred_element_type=jnp.float32)
        * softmax_scale
    )
    mask_heads = allowed[:, None, :]
    new_max = jnp.maximum(running_max, jnp.max(jnp.where(mask_heads, scores, -1e30), axis=-1))
    weights = jnp.where(mask_heads, jnp.exp(scores - new_max[..., None]), 0.0)
    rescale = jnp.exp(running_max - new_max)
    totals = totals * rescale + jnp.sum(weights, axis=-1)
    output_acc = output_acc * rescale[..., None] + jnp.einsum(
        "qhk,khd->qhd",
        weights.astype(jnp.bfloat16),
        value_heads,
        preferred_element_type=jnp.float32,
    )
    return (output_acc, new_max, totals)


def process_shard(
    carry_state, query_heads, query_clip, query_frame, pair_rows, key_start, clip_ids
):
    return attend_tile(
        carry_state, query_heads, query_clip, query_frame, pair_rows, key_start, clip_ids
    )


def per_device(queries, keys, values, clip_ids):
    tok_rows = queries.shape[0]
    width_all = queries.shape[1]
    head_count = width_all // HEAD_DIM
    devices = lax.axis_size("ctx")
    reach = min(8, devices) - 1
    first_row = lax.axis_index("ctx") * tok_rows
    query_clip = lax.dynamic_slice_in_dim(clip_ids, first_row, tok_rows, 0)
    query_frame = (first_row + jnp.arange(tok_rows, dtype=jnp.int32)) // FRAME
    query_heads = queries.reshape(tok_rows, head_count, HEAD_DIM)
    carry_state = (
        jnp.zeros((tok_rows, head_count, HEAD_DIM), jnp.float32),
        jnp.full((tok_rows, head_count), -1e30, jnp.float32),
        jnp.zeros((tok_rows, head_count), jnp.float32),
    )
    paired = jnp.stack([keys, values])
    carry_state = process_shard(
        carry_state, query_heads, query_clip, query_frame, paired, first_row, clip_ids
    )

    def advance(loop_index, loop_state):
        inner_state, moving = loop_state
        moving = from_behind(moving, "ctx", 1)
        key_start = first_row - (loop_index + 1) * tok_rows
        inner_state = process_shard(
            inner_state, query_heads, query_clip, query_frame, moving, key_start, clip_ids
        )
        return (inner_state, moving)

    carry_state, paired = lax.fori_loop(0, reach, advance, (carry_state, paired))
    output_acc, running_max, totals = carry_state
    attended = output_acc / totals[..., None]
    return attended.reshape(tok_rows, width_all).astype(jnp.bfloat16)


def solution(mesh):
    placed = (P(("dp", "ctx"), None), P(("dp", "ctx"), None), P(("dp", "ctx"), None), P("dp"))
    return jax.shard_map(
        per_device, mesh=mesh, in_specs=placed, out_specs=P(("dp", "ctx"), None), check_vma=False
    )
```

profile of v0, /device:TPU:24, one launch (start us, length us, event | category | flops | bytes accessed | tf_op | source)
XLA Modules:
  0.0 293.5 jit_solution(16121942924521953763)
XLA Ops:
  0.0 0.8 fusion.51
  1.2 1.5 copy.13
  2.7 0.7 copy.20
  3.4 1.5 copy.18
  4.9 2.3 copy.19
  7.2 2.7 pad_maximum_fusion
  9.9 2.9 fusion.24
  12.8 1.7 fusion.27
  14.6 4.2 %bitcast_add_fusion.1 = f32[512,8,128]{2,0,1:T(8,128)} fusion(f32[8,512,512]{2,1,0:T(8,128)S(1)} %get-tuple-element.336, f32[512,8]{0,1:T(8,128)S(1)} %broadcast_maximum_fusion, pred[512,512]{0,1:T(8,128)(4,1)S(1)} %compare_and_fusion.1, f32[512,8]{0,1:T(8,128)S(1)} %get-tuple-element.334, bf16[512,1024]{1,0:T(8,128)(2,1)S(1)} %copy-done.2), kind=kOutput, calls=%fused_computation.51 | convolution fusion | flops 545783808 | bytes 11829248 | tf_op jit(solution)/shard_map/qhk,khd->qhd/dot_general | solution.py:42
  18.8 271.9 %while.23 = (s32[]{:T(128)}, f32[512,8,128]{2,0,1:T(8,128)}, f32[512,8]{0,1:T(8,128)S(1)}, f32[512,8]{0,1:T(8,128)S(1)}, bf16[2,512,1024]{1,2,0:T(8,128)(2,1)}, ...) while((s32[]{:T(128)}, f32[512,8,128]{2,0,1:T(8,128)}, ...), condition=%wide.region_5.6_spmd.clone.clone, body=%wide.region_2.5_spmd.clone.clone.sunk | while | flops 1098933248 | bytes 67388680 | solution.py:88
  18.8 1.9 collective-permute-start
  20.7 0.8 dynamic_slice.23
  21.9 28.2 %collective-permute-done = bf16[2,512,1024]{1,2,0:T(8,128)(2,1)S(1)} collective-permute-done((bf16[2,512,1024]{1,2,0:T(8,128)(2,1)}, bf16[2,512,1024]{1,2,0:T(8,128)(2,1)S(1)}, u32[]{:S(2)}, u32[]{:S(2)}) %collective-permute-start) | collective-permute-done | bytes 2097184 | tf_op jit(solution)/shard_map/while/body/eval_jaxpr/ppermute | solution.py:15
  50.3 1.7 fusion.73
  52.0 1.7 fusion.74
  53.7 3.3 %bitcast_add_fusion.3 = f32[512,8,128]{2,0,1:T(8,128)S(1)} fusion(f32[512,8,128]{2,0,1:T(8,128)S(1)} %copy-done, bf16[512,8,128]{0,2,1:T(8,128)(2,1)S(1)} %bitcast.85, f32[8,512,512]{2,1,0:T(8,128)S(1)} %get-tuple-element.405, f32[512,8]{0,1:T(8,128)S(1)} %max.31, pred[512,512]{0,1:T(8,128)(4,1)S(1)} %compare_and_fusion.3, ...), kind=kOutput, calls=%fused_computation.13.clone.1 | convolution fusion | flops 546308096 | bytes 13926400 | tf_op jit(solution)/shard_map/while/body/eval_jaxpr/qhk,khd->qhd/dot_general | solution.py:42
  57.1 1.3 copy.55
  58.4 0.6 copy-done.1
  59.1 1.9 collective-permute-start
  61.0 0.8 dynamic_slice.23
  62.1 26.6 %collective-permute-done = bf16[2,512,1024]{1,2,0:T(8,128)(2,1)S(1)} collective-permute-done((bf16[2,512,1024]{1,2,0:T(8,128)(2,1)}, bf16[2,512,1024]{1,2,0:T(8,128)(2,1)S(1)}, u32[]{:S(2)}, u32[]{:S(2)}) %collective-permute-start) | collective-permute-done | bytes 2097184 | tf_op jit(solution)/shard_map/while/body/eval_jaxpr/ppermute | solution.py:15
  88.9 1.7 fusion.73
  90.6 1.7 fusion.74
  92.4 3.3 %bitcast_add_fusion.3 = f32[512,8,128]{2,0,1:T(8,128)S(1)} fusion(f32[512,8,128]{2,0,1:T(8,128)S(1)} %copy-done, bf16[512,8,128]{0,2,1:T(8,128)(2,1)S(1)} %bitcast.85, f32[8,512,512]{2,1,0:T(8,128)S(1)} %get-tuple-element.405, f32[512,8]{0,1:T(8,128)S(1)} %max.31, pred[512,512]{0,1:T(8,128)(4,1)S(1)} %compare_and_fusion.3, ...), kind=kOutput, calls=%fused_computation.13.clone.1 | convolution fusion | flops 546308096 | bytes 13926400 | tf_op jit(solution)/shard_map/while/body/eval_jaxpr/qhk,khd->qhd/dot_general | solution.py:42
  95.7 1.3 copy.55
  97.0 0.6 copy-done.1
  97.7 1.9 collective-permute-start
  99.6 0.8 dynamic_slice.23
  100.7 26.6 %collective-permute-done = bf16[2,512,1024]{1,2,0:T(8,128)(2,1)S(1)} collective-permute-done((bf16[2,512,1024]{1,2,0:T(8,128)(2,1)}, bf16[2,512,1024]{1,2,0:T(8,128)(2,1)S(1)}, u32[]{:S(2)}, u32[]{:S(2)}) %collective-permute-start) | collective-permute-done | bytes 2097184 | tf_op jit(solution)/shard_map/while/body/eval_jaxpr/ppermute | solution.py:15
  127.5 1.7 fusion.73
  129.2 1.7 fusion.74
  131.0 3.3 %bitcast_add_fusion.3 = f32[512,8,128]{2,0,1:T(8,128)S(1)} fusion(f32[512,8,128]{2,0,1:T(8,128)S(1)} %copy-done, bf16[512,8,128]{0,2,1:T(8,128)(2,1)S(1)} %bitcast.85, f32[8,512,512]{2,1,0:T(8,128)S(1)} %get-tuple-element.405, f32[512,8]{0,1:T(8,128)S(1)} %max.31, pred[512,512]{0,1:T(8,128)(4,1)S(1)} %compare_and_fusion.3, ...), kind=kOutput, calls=%fused_computation.13.clone.1 | convolution fusion | flops 546308096 | bytes 13926400 | tf_op jit(solution)/shard_map/while/body/eval_jaxpr/qhk,khd->qhd/dot_general | solution.py:42
  134.3 1.3 copy.55
  135.7 0.6 copy-done.1
  136.3 1.9 collective-permute-start
  138.2 0.8 dynamic_slice.23
  139.4 26.6 %collective-permute-done = bf16[2,512,1024]{1,2,0:T(8,128)(2,1)S(1)} collective-permute-done((bf16[2,512,1024]{1,2,0:T(8,128)(2,1)}, bf16[2,512,1024]{1,2,0:T(8,128)(2,1)S(1)}, u32[]{:S(2)}, u32[]{:S(2)}) %collective-permute-start) | collective-permute-done | bytes 2097184 | tf_op jit(solution)/shard_map/while/body/eval_jaxpr/ppermute | solution.py:15
  166.1 1.7 fusion.73
  167.8 1.7 fusion.74
  169.6 3.3 %bitcast_add_fusion.3 = f32[512,8,128]{2,0,1:T(8,128)S(1)} fusion(f32[512,8,128]{2,0,1:T(8,128)S(1)} %copy-done, bf16[512,8,128]{0,2,1:T(8,128)(2,1)S(1)} %bitcast.85, f32[8,512,512]{2,1,0:T(8,128)S(1)} %get-tuple-element.405, f32[512,8]{0,1:T(8,128)S(1)} %max.31, pred[512,512]{0,1:T(8,128)(4,1)S(1)} %compare_and_fusion.3, ...), kind=kOutput, calls=%fused_computation.13.clone.1 | convolution fusion | flops 546308096 | bytes 13926400 | tf_op jit(solution)/shard_map/while/body/eval_jaxpr/qhk,khd->qhd/dot_general | solution.py:42
  172.9 1.3 copy.55
  174.3 0.6 copy-done.1
  174.9 1.9 collective-permute-start
  176.8 0.8 dynamic_slice.23
  178.0 26.6 %collective-permute-done = bf16[2,512,1024]{1,2,0:T(8,128)(2,1)S(1)} collective-permute-done((bf16[2,512,1024]{1,2,0:T(8,128)(2,1)}, bf16[2,512,1024]{1,2,0:T(8,128)(2,1)S(1)}, u32[]{:S(2)}, u32[]{:S(2)}) %collective-permute-start) | collective-permute-done | bytes 2097184 | tf_op jit(solution)/shard_map/while/body/eval_jaxpr/ppermute | solution.py:15
  204.7 1.7 fusion.73
  206.4 1.7 fusion.74
  208.2 3.3 %bitcast_add_fusion.3 = f32[512,8,128]{2,0,1:T(8,128)S(1)} fusion(f32[512,8,128]{2,0,1:T(8,128)S(1)} %copy-done, bf16[512,8,128]{0,2,1:T(8,128)(2,1)S(1)} %bitcast.85, f32[8,512,512]{2,1,0:T(8,128)S(1)} %get-tuple-element.405, f32[512,8]{0,1:T(8,128)S(1)} %max.31, pred[512,512]{0,1:T(8,128)(4,1)S(1)} %compare_and_fusion.3, ...), kind=kOutput, calls=%fused_computation.13.clone.1 | convolution fusion | flops 546308096 | bytes 13926400 | tf_op jit(solution)/shard_map/while/body/eval_jaxpr/qhk,khd->qhd/dot_general | solution.py:42
  211.5 1.3 copy.55
  213.5 1.9 collective-permute-start
  215.4 0.8 dynamic_slice.23
  216.6 26.6 %collective-permute-done = bf16[2,512,1024]{1,2,0:T(8,128)(2,1)S(1)} collective-permute-done((bf16[2,512,1024]{1,2,0:T(8,128)(2,1)}, bf16[2,512,1024]{1,2,0:T(8,128)(2,1)S(1)}, u32[]{:S(2)}, u32[]{:S(2)}) %collective-permute-start) | collective-permute-done | bytes 2097184 | tf_op jit(solution)/shard_map/while/body/eval_jaxpr/ppermute | solution.py:15
  243.3 1.7 fusion.73
  245.0 1.7 fusion.74
  246.8 3.3 %bitcast_add_fusion.3 = f32[512,8,128]{2,0,1:T(8,128)S(1)} fusion(f32[512,8,128]{2,0,1:T(8,128)S(1)} %copy-done, bf16[512,8,128]{0,2,1:T(8,128)(2,1)S(1)} %bitcast.85, f32[8,512,512]{2,1,0:T(8,128)S(1)} %get-tuple-element.405, f32[512,8]{0,1:T(8,128)S(1)} %max.31, pred[512,512]{0,1:T(8,128)(4,1)S(1)} %compare_and_fusion.3, ...), kind=kOutput, calls=%fused_computation.13.clone.1 | convolution fusion | flops 546308096 | bytes 13926400 | tf_op jit(solution)/shard_map/while/body/eval_jaxpr/qhk,khd->qhd/dot_general | solution.py:42
  250.1 1.3 copy.55
  252.1 1.9 collective-permute-start
  254.0 0.8 dynamic_slice.23
  255.2 26.6 %collective-permute-done = bf16[2,512,1024]{1,2,0:T(8,128)(2,1)S(1)} collective-permute-done((bf16[2,512,1024]{1,2,0:T(8,128)(2,1)}, bf16[2,512,1024]{1,2,0:T(8,128)(2,1)S(1)}, u32[]{:S(2)}, u32[]{:S(2)}) %collective-permute-start) | collective-permute-done | bytes 2097184 | tf_op jit(solution)/shard_map/while/body/eval_jaxpr/ppermute | solution.py:15
  281.9 1.7 fusion.73
  283.6 1.7 fusion.74
  285.4 3.3 %bitcast_add_fusion.3 = f32[512,8,128]{2,0,1:T(8,128)S(1)} fusion(f32[512,8,128]{2,0,1:T(8,128)S(1)} %copy-done, bf16[512,8,128]{0,2,1:T(8,128)(2,1)S(1)} %bitcast.85, f32[8,512,512]{2,1,0:T(8,128)S(1)} %get-tuple-element.405, f32[512,8]{0,1:T(8,128)S(1)} %max.31, pred[512,512]{0,1:T(8,128)(4,1)S(1)} %compare_and_fusion.3, ...), kind=kOutput, calls=%fused_computation.13.clone.1 | convolution fusion | flops 546308096 | bytes 13926400 | tf_op jit(solution)/shard_map/while/body/eval_jaxpr/qhk,khd->qhd/dot_general | solution.py:42
  288.8 1.3 copy.55
  290.7 2.7 copy_bitcast_fusion
  (79 shorter events, 5.9 us)
Async XLA Ops:
  9.9 4.7 %copy-start.2 = (bf16[512,1024]{1,0:T(8,128)(2,1)S(1)}, bf16[512,1024]{1,0:T(8,128)(2,1)}, u32[]{:S(2)}) copy-start(bf16[512,1024]{1,0:T(8,128)(2,1)} %param.8) | copy-start | bytes 3145732
  18.8 31.3 %collective-permute-start = (bf16[2,512,1024]{1,2,0:T(8,128)(2,1)}, bf16[2,512,1024]{1,2,0:T(8,128)(2,1)S(1)}, u32[]{:S(2)}, u32[]{:S(2)}) collective-permute-start(bf16[2,512,1024]{1,2,0:T(8,128)(2,1)} %get-tuple-element.425), channel_id=1, source_target_pairs={{0,1},{1,2},{2,3},{3,4},{4,5},{5,6},{6,7},{7,8},{8,9},{9,10},{10,1... | collective-permute-start | bytes 6291464 | tf_op jit(solution)/shard_map/while/body/eval_jaxpr/ppermute | solution.py:15
  50.2 3.5 %copy-start = (f32[512,8,128]{2,0,1:T(8,128)S(1)}, f32[512,8,128]{2,0,1:T(8,128)}, u32[]{:S(2)}) copy-start(f32[512,8,128]{2,0,1:T(8,128)} %get-tuple-element.422) | copy-start | bytes 6291460 | tf_op jit(solution)/shard_map/while
  57.1 2.0 copy-start.1
  59.1 29.7 %collective-permute-start = (bf16[2,512,1024]{1,2,0:T(8,128)(2,1)}, bf16[2,512,1024]{1,2,0:T(8,128)(2,1)S(1)}, u32[]{:S(2)}, u32[]{:S(2)}) collective-permute-start(bf16[2,512,1024]{1,2,0:T(8,128)(2,1)} %get-tuple-element.425), channel_id=1, source_target_pairs={{0,1},{1,2},{2,3},{3,4},{4,5},{5,6},{6,7},{7,8},{8,9},{9,10},{10,1... | collective-permute-start | bytes 6291464 | tf_op jit(solution)/shard_map/while/body/eval_jaxpr/ppermute | solution.py:15
  88.9 3.5 %copy-start = (f32[512,8,128]{2,0,1:T(8,128)S(1)}, f32[512,8,128]{2,0,1:T(8,128)}, u32[]{:S(2)}) copy-start(f32[512,8,128]{2,0,1:T(8,128)} %get-tuple-element.422) | copy-start | bytes 6291460 | tf_op jit(solution)/shard_map/while
  95.7 2.0 copy-start.1
  97.7 29.7 %collective-permute-start = (bf16[2,512,1024]{1,2,0:T(8,128)(2,1)}, bf16[2,512,1024]{1,2,0:T(8,128)(2,1)S(1)}, u32[]{:S(2)}, u32[]{:S(2)}) collective-permute-start(bf16[2,512,1024]{1,2,0:T(8,128)(2,1)} %get-tuple-element.425), channel_id=1, source_target_pairs={{0,1},{1,2},{2,3},{3,4},{4,5},{5,6},{6,7},{7,8},{8,9},{9,10},{10,1... | collective-permute-start | bytes 6291464 | tf_op jit(solution)/shard_map/while/body/eval_jaxpr/ppermute | solution.py:15
  127.5 3.5 %copy-start = (f32[512,8,128]{2,0,1:T(8,128)S(1)}, f32[512,8,128]{2,0,1:T(8,128)}, u32[]{:S(2)}) copy-start(f32[512,8,128]{2,0,1:T(8,128)} %get-tuple-element.422) | copy-start | bytes 6291460 | tf_op jit(solution)/shard_map/while
  134.3 2.0 copy-start.1
  136.3 29.7 %collective-permute-start = (bf16[2,512,1024]{1,2,0:T(8,128)(2,1)}, bf16[2,512,1024]{1,2,0:T(8,128)(2,1)S(1)}, u32[]{:S(2)}, u32[]{:S(2)}) collective-permute-start(bf16[2,512,1024]{1,2,0:T(8,128)(2,1)} %get-tuple-element.425), channel_id=1, source_target_pairs={{0,1},{1,2},{2,3},{3,4},{4,5},{5,6},{6,7},{7,8},{8,9},{9,10},{10,1... | collective-permute-start | bytes 6291464 | tf_op jit(solution)/shard_map/while/body/eval_jaxpr/ppermute | solution.py:15
  166.1 3.5 %copy-start = (f32[512,8,128]{2,0,1:T(8,128)S(1)}, f32[512,8,128]{2,0,1:T(8,128)}, u32[]{:S(2)}) copy-start(f32[512,8,128]{2,0,1:T(8,128)} %get-tuple-element.422) | copy-start | bytes 6291460 | tf_op jit(solution)/shard_map/while
  172.9 2.0 copy-start.1
  174.9 29.7 %collective-permute-start = (bf16[2,512,1024]{1,2,0:T(8,128)(2,1)}, bf16[2,512,1024]{1,2,0:T(8,128)(2,1)S(1)}, u32[]{:S(2)}, u32[]{:S(2)}) collective-permute-start(bf16[2,512,1024]{1,2,0:T(8,128)(2,1)} %get-tuple-element.425), channel_id=1, source_target_pairs={{0,1},{1,2},{2,3},{3,4},{4,5},{5,6},{6,7},{7,8},{8,9},{9,10},{10,1... | collective-permute-start | bytes 6291464 | tf_op jit(solution)/shard_map/while/body/eval_jaxpr/ppermute | solution.py:15
  204.7 3.5 %copy-start = (f32[512,8,128]{2,0,1:T(8,128)S(1)}, f32[512,8,128]{2,0,1:T(8,128)}, u32[]{:S(2)}) copy-start(f32[512,8,128]{2,0,1:T(8,128)} %get-tuple-element.422) | copy-start | bytes 6291460 | tf_op jit(solution)/shard_map/while
  211.5 2.0 copy-start.1
  213.5 29.7 %collective-permute-start = (bf16[2,512,1024]{1,2,0:T(8,128)(2,1)}, bf16[2,512,1024]{1,2,0:T(8,128)(2,1)S(1)}, u32[]{:S(2)}, u32[]{:S(2)}) collective-permute-start(bf16[2,512,1024]{1,2,0:T(8,128)(2,1)} %get-tuple-element.425), channel_id=1, source_target_pairs={{0,1},{1,2},{2,3},{3,4},{4,5},{5,6},{6,7},{7,8},{8,9},{9,10},{10,1... | collective-permute-start | bytes 6291464 | tf_op jit(solution)/shard_map/while/body/eval_jaxpr/ppermute | solution.py:15
  243.3 3.5 %copy-start = (f32[512,8,128]{2,0,1:T(8,128)S(1)}, f32[512,8,128]{2,0,1:T(8,128)}, u32[]{:S(2)}) copy-start(f32[512,8,128]{2,0,1:T(8,128)} %get-tuple-element.422) | copy-start | bytes 6291460 | tf_op jit(solution)/shard_map/while
  250.1 2.0 copy-start.1
  252.1 29.7 %collective-permute-start = (bf16[2,512,1024]{1,2,0:T(8,128)(2,1)}, bf16[2,512,1024]{1,2,0:T(8,128)(2,1)S(1)}, u32[]{:S(2)}, u32[]{:S(2)}) collective-permute-start(bf16[2,512,1024]{1,2,0:T(8,128)(2,1)} %get-tuple-element.425), channel_id=1, source_target_pairs={{0,1},{1,2},{2,3},{3,4},{4,5},{5,6},{6,7},{7,8},{8,9},{9,10},{10,1... | collective-permute-start | bytes 6291464 | tf_op jit(solution)/shard_map/while/body/eval_jaxpr/ppermute | solution.py:15
  281.9 3.5 %copy-start = (f32[512,8,128]{2,0,1:T(8,128)S(1)}, f32[512,8,128]{2,0,1:T(8,128)}, u32[]{:S(2)}) copy-start(f32[512,8,128]{2,0,1:T(8,128)} %get-tuple-element.422) | copy-start | bytes 6291460 | tf_op jit(solution)/shard_map/while
  288.7 2.0 copy-start.1
where the time goes:
time: 294 us; the launch traced here: 293 us
  waiting for transfers between devices  188 us (64%)
  matrix products  42.3 us (14%)
  local copies, waits for them, and re-layouts  26.1 us (9%)
  other arithmetic  23.1 us (8%)
  starting transfers between devices  13.4 us (5%)
    ppermute x7, waiting for transfers between devices, from_behind(): return lax.ppermute(x, axis, pairs)  188 us
    dot_general x8, matrix products, attend_tile(): jnp.einsum('qhk,khd->qhd', weights.astype(jnp.bfloat16), value_heads, pre...  27.5 us
    dot_general x8, matrix products, attend_tile(): jnp.einsum('qhd,khd->qhk', query_heads, key_heads, preferred_element_type...  14.7 us
    reduce_sum x8, other arithmetic, attend_tile(): totals = totals * rescale + jnp.sum(weights, axis=-1)  13.8 us
    while x42, local copies, waits for them, and re-layouts  13.8 us
    ppermute x7, starting transfers between devices, from_behind(): return lax.ppermute(x, axis, pairs)  13.4 us
    unnamed x6, local copies, waits for them, and re-layouts  5.94 us
  transfers between devices with their start and end apart: 7, of which 7 were waited for; matrix products, arithmetic and copies ran while one was open for 3% of the time, Pallas kernels for 0%

commit v1 on v0

v1 whole, which is shorter than its diff:
```python
import functools
import math

import jax
import jax.numpy as jnp
from jax import lax
from jax.experimental import pallas as pl
from jax.experimental.pallas import tpu as pltpu
from jax.sharding import PartitionSpec as P

HEAD_DIM = 128
FRAME = 256
MESH = pl.DeviceIdType.MESH
F32 = jnp.float32
BF16 = jnp.bfloat16

CHIP = 1024
HALF = 512
LANE_HEADS = 4
WIDTH = LANE_HEADS * HEAD_DIM
T = 128
K = CHIP // T
HOPS = 3
PENALTY = 16384.0
SCALE = math.log2(math.e) / math.sqrt(HEAD_DIM)


def nt_dot(a, b):
    return lax.dot_general(a, b, (((1,), (1,)), ((), ())), preferred_element_type=F32)


def attend(q, qa, key_of, value_of, key_mask, lse_in, out_in):
    rows = q.shape[0]
    lane = lax.broadcasted_iota(jnp.int32, (rows, 128), 1)
    stats = jnp.zeros((rows, 128), F32)
    outs = []
    for h in range(LANE_HEADS):
        cols = slice(h * HEAD_DIM, (h + 1) * HEAD_DIM)
        scores = nt_dot(
            jnp.concatenate([q[:, cols], qa], axis=1),
            jnp.concatenate([key_of(cols), key_mask], axis=1),
        )
        top = jnp.max(scores, axis=1, keepdims=True) * SCALE
        if lse_in is not None:
            before = lse_in[:, h : h + 1]
            top = jnp.maximum(top, before)
        weights = jnp.exp2(scores * SCALE - top).astype(BF16)
        values = value_of(cols)
        both = jnp.dot(
            weights,
            jnp.concatenate([values, jnp.ones_like(values)], axis=1),
            preferred_element_type=F32,
        )
        mixed, total = both[:, :HEAD_DIM], both[:, HEAD_DIM:]
        if lse_in is not None:
            keep = jnp.exp2(before - top)
            mixed = mixed + out_in[:, cols].astype(F32) * keep
            total = total + keep
        outs.append((mixed / total).astype(BF16))
        stats = jnp.where(lane == h, top + jnp.log2(total), stats)
    return outs, stats


def kernel(
    q_ref, k_ref, v_ref, clip_ref, out_ref,
    qb, kb, vb, kl, vl, qa, ka, kla, oin, oout, lin, lout, cw,
    load_sem, clip_sem, sib_send, sib_recv, left_send, left_recv,
    q_send, q_recv, o_send, o_recv, l_send, l_recv, out_sem, out_send, out_recv,
):
    size = lax.axis_size("ctx")
    chips = size // 2
    me = lax.axis_index("ctx")
    core = lax.rem(me, 2)
    chip = me // 2
    sib = chip * 2 + (1 - core)
    prev = lax.rem(me + size - 2, size)
    nxt = lax.rem(me + 2, size)

    def remote(src, dst, send, recv, to):
        return pltpu.make_async_remote_copy(
            src_ref=src, dst_ref=dst, send_sem=send, recv_sem=recv,
            device_id={"ctx": to}, device_id_type=MESH,
        )

    mine = pl.ds(pl.multiple_of(core * HALF, HALF), HALF)
    theirs = pl.ds(pl.multiple_of((1 - core) * HALF, HALF), HALF)
    whole = pl.ds(0, HALF)

    loads = [
        pltpu.make_async_copy(src.at[whole, mine], dst, load_sem.at[i])
        for i, (src, dst) in enumerate(
            [(q_ref, qb.at[0, mine]), (k_ref, kb.at[mine]), (v_ref, vb.at[mine])]
        )
    ]
    for copy in loads:
        copy.start()
    clips = []
    for i in range(HOPS + 2):
        row = pl.multiple_of(lax.rem(chip + chips - 1 + i, chips) * 8, 8)
        clips.append(
            pltpu.make_async_copy(clip_ref.at[pl.ds(row, 8)], cw.at[pl.ds(8 * i, 8)], clip_sem.at[i])
        )
    for copy in clips:
        copy.start()

    barrier = pltpu.get_barrier_semaphore()
    for to in (sib, prev, nxt):
        pl.semaphore_signal(barrier, inc=1, device_id={"ctx": to}, device_id_type=MESH)
    pl.semaphore_wait(barrier, 3)

    swaps = [
        remote(src.at[whole, theirs], dst, sib_send.at[i], sib_recv.at[i], sib)
        for i, (src, dst) in enumerate(
            [(q_ref, qb.at[0, mine]), (k_ref, kb.at[mine]), (v_ref, vb.at[mine])]
        )
    ]
    for copy in swaps:
        copy.start()

    def rows_of(k):
        return pl.ds(pl.multiple_of(lax.rem(k + K // 2, K) * T, T), T)

    def send_q(d, k):
        r = rows_of(k)
        return remote(qb.at[d - 1, r], qb.at[d, r], q_send.at[d - 1, k], q_recv.at[d - 1, k], prev)

    def send_o(d, k):
        r = rows_of(k)
        return remote(oout.at[d, r], oin.at[d - 1, r], o_send.at[d - 1, k], o_recv.at[d - 1, k], nxt)

    def send_l(d, k):
        return remote(lout.at[d, k], lin.at[d - 1, k], l_send.at[d - 1, k], l_recv.at[d - 1, k], nxt)

    loads[0].wait()
    swaps[0].wait_recv()
    send_q(1, 0).start()

    for i in (1, 2):
        loads[i].wait()
        swaps[i].wait_recv()
    late = pl.ds(HALF, HALF)
    lefts = [
        remote(kb.at[late], kl, left_send.at[0], left_recv.at[0], nxt),
        remote(vb.at[late], vl, left_send.at[1], left_recv.at[1], nxt),
    ]
    for copy in lefts:
        copy.start()

    for copy in clips:
        copy.wait()
    lane = lax.broadcasted_iota(jnp.int32, (128, 128), 1)

    def clip_columns(row):
        wide = jnp.broadcast_to(cw[pl.ds(row, 1), :].astype(F32), (128, 128))
        return wide.T.astype(jnp.int32)

    @pl.loop(0, 4)
    def _(i):
        same = clip_columns(4 + i) == lane
        kla[pl.ds(pl.multiple_of(i * 128, 128), 128), :] = jnp.where(
            same | (lane >= 32), 0.0, -PENALTY
        ).astype(BF16)

    @pl.loop(0, 8)
    def _(i):
        same = clip_columns(8 + i) == lane
        frame = i // (FRAME // 128)
        r = pl.ds(pl.multiple_of(i * 128, 128), 128)
        later = (lane >= 32) & (frame > lane - 32)
        ka[r, :] = jnp.where((~same & (lane < 32)) | later, -PENALTY, 0.0).astype(BF16)
        qa[0, r, :] = jnp.where(same | (lane == 32 + frame), 1.0, 0.0).astype(BF16)

    @pl.loop(0, 8 * HOPS)
    def _(i):
        same = clip_columns(16 + i) == lane
        r = pl.ds(pl.multiple_of(lax.rem(i, 8) * 128, 128), 128)
        qa[1 + i // 8, r, :] = jnp.where(same, 1.0, 0.0).astype(BF16)

    oin[HOPS] = jnp.zeros((CHIP, WIDTH), BF16)
    lin[HOPS] = jnp.full((K, 8, T), -1e30, F32)

    def store_stats(ref, d, k, stats):
        ref[d, k] = stats.T[:8, :]

    @pl.loop(0, K + 2 * HOPS)
    def _(j):
        @pl.when((j >= 1) & (j < K))
        def _():
            send_q(1, j).start()

        for hop in range(1, HOPS):
            @pl.when((j >= hop) & (j < K + hop))
            def _(hop=hop):
                send_q(hop, j - hop).wait_recv()
                send_q(hop + 1, j - hop).start()

        @pl.when((j >= HOPS) & (j < K + HOPS))
        def _():
            k = j - HOPS
            send_q(HOPS, k).wait_recv()

            @pl.when(k == K // 2)
            def _():
                for copy in lefts:
                    copy.wait_recv()

            @pl.when(k >= K // 2)
            def _():
                r = rows_of(k)
                outs, stats = attend(
                    qb[HOPS, r, :], qa[HOPS, r, :],
                    lambda cols: kl[:, cols], lambda cols: vl[:, cols], kla[...], None, None,
                )
                oin[HOPS, r, :] = jnp.concatenate(outs, axis=1)
                store_stats(lin, HOPS, k, stats)

        @pl.loop(0, HOPS + 1)
        def _(back):
            d = HOPS - back
            k = j - HOPS - back

            @pl.when((k >= 0) & (k < K))
            def _():
                @pl.when(d < HOPS)
                def _():
                    send_o(d + 1, k).wait_recv()
                    send_l(d + 1, k).wait_recv()

                r = rows_of(k)
                lse = jnp.concatenate([lin[d, k], jnp.zeros((120, T), F32)], axis=0).T
                outs, stats = attend(
                    qb[d, r, :], qa[d, r, :],
                    lambda cols: kb[:, cols], lambda cols: vb[:, cols], ka[...], lse, oin[d, r, :],
                )
                oout[d, r, :] = jnp.concatenate(outs, axis=1)
                store_stats(lout, d, k, stats)

                @pl.when(d > 0)
                def _():
                    send_o(d, k).start()
                    send_l(d, k).start()

    here = pltpu.make_async_copy(oout.at[0, mine], out_ref.at[whole, mine], out_sem)
    there = remote(oout.at[0, theirs], out_ref.at[whole, mine], out_send, out_recv, sib)
    there.start()
    here.start()

    for copy in swaps + lefts:
        copy.wait_send()

    @pl.loop(0, K)
    def _(k):
        for d in range(1, HOPS + 1):
            send_q(d, k).wait_send()
            send_o(d, k).wait_send()
            send_l(d, k).wait_send()

    here.wait()
    there.wait()


def per_device(queries, keys, values, clip_ids):
    tokens, width = queries.shape
    anywhere = pl.BlockSpec(memory_space=pl.ANY)
    dma = pltpu.SemaphoreType.DMA
    return pl.pallas_call(
        kernel,
        out_shape=jax.ShapeDtypeStruct((tokens, width), BF16),
        in_specs=[anywhere] * 4,
        out_specs=anywhere,
        scratch_shapes=[
            pltpu.VMEM((HOPS + 1, CHIP, WIDTH), BF16),
            pltpu.VMEM((CHIP, WIDTH), BF16),
            pltpu.VMEM((CHIP, WIDTH), BF16),
            pltpu.VMEM((HALF, WIDTH), BF16),
            pltpu.VMEM((HALF, WIDTH), BF16),
            pltpu.VMEM((HOPS + 1, CHIP, 128), BF16),
            pltpu.VMEM((CHIP, 128), BF16),
            pltpu.VMEM((HALF, 128), BF16),
            pltpu.VMEM((HOPS + 1, CHIP, WIDTH), BF16),
            pltpu.VMEM((HOPS + 1, CHIP, WIDTH), BF16),
            pltpu.VMEM((HOPS + 1, K, 8, T), F32),
            pltpu.VMEM((HOPS + 1, K, 8, T), F32),
            pltpu.VMEM((8 * (HOPS + 2), 128), jnp.int32),
            dma((3,)), dma((HOPS + 2,)), dma((3,)), dma((3,)), dma((2,)), dma((2,)),
            dma((HOPS, K)), dma((HOPS, K)), dma((HOPS, K)), dma((HOPS, K)),
            dma((HOPS, K)), dma((HOPS, K)),
            dma, dma, dma,
        ],
        compiler_params=pltpu.CompilerParams(
            collective_id=0, has_side_effects=True, vmem_limit_bytes=48 << 20
        ),
        name="chain_attention",
    )(queries, keys, values, clip_ids.reshape(-1, 128))


def solution(mesh):
    placed = (P(("dp", "ctx"), None), P(("dp", "ctx"), None), P(("dp", "ctx"), None), P("dp"))
    return jax.shard_map(
        per_device, mesh=mesh, in_specs=placed, out_specs=P(("dp", "ctx"), None), check_vma=False
    )
```

time: 294 us -> 140 us (0.48)
  the two profiles are of different devices: /device:TPU:24 before, /device:TPU:1 now
where the time goes in v1:
time: 140 us
  Pallas kernels  134 us (96%)
  local copies, waits for them, and re-layouts  5.55 us (4%)
    pallas_call x1, Pallas kernels, per_device(): pl.pallas_call(kernel, out_shape=jax.ShapeDtypeStruct((tokens, width), BF...  134 us
    unnamed x9, local copies, waits for them, and re-layouts  5.55 us

profile of v1, /device:TPU:1, one launch (start us, length us, event | category | flops | bytes accessed | tf_op | source)
XLA Modules:
  0.0 139.6 jit_solution(16848131776214532412)
XLA Ops:
  0.0 0.0 copy-start
  0.0 1.2 copy-done
  1.2 0.0 copy-start.1
  1.2 1.2 copy-done.1
  2.5 0.0 copy-start.2
  2.5 1.2 copy-done.2
  3.7 0.0 copy-start.3
  3.7 0.9 copy-done.3
  4.6 134.0 %chain_attention.1 = bf16[512,1024]{1,0:T(8,128)(2,1)S(1)} custom-call(bf16[512,1024]{1,0:T(8,128)(2,1)S(1)} %copy-done, bf16[512,1024]{1,0:T(8,128)(2,1)S(1)} %copy-done.1, bf16[512,1024]{1,0:T(8,128)(2,1)S(1)} %copy-done.2, s32[256,128]{1,0:T(8,128)S(1)} %bitcast.1), custom_call_target="tpu_custom_call" | custom-call | tf_op jit(solution)/shard_map/chain_attention/pallas_call | solution.py:266
  138.6 1.0 copy.6
Async XLA Ops:
  0.0 1.2 copy-start
  1.2 1.2 copy-start.1
  2.5 1.2 copy-start.2
  3.7 0.9 copy-start.3

commit v2 on v0

v2 whole, which is shorter than its diff:
```python
import functools
import math

import jax
import jax.numpy as jnp
from jax import lax
from jax.experimental import pallas as pl
from jax.experimental.pallas import tpu as pltpu
from jax.sharding import PartitionSpec as P

HEAD_DIM = 128
FRAME = 256
MESH = pl.DeviceIdType.MESH
F32 = jnp.float32
BF16 = jnp.bfloat16

CHIP = 1024
HALF = 512
LANE_HEADS = 4
WIDTH = LANE_HEADS * HEAD_DIM
T = 128
K = CHIP // T
HOPS = 3
PENALTY = 16384.0
SCALE = math.log2(math.e) / math.sqrt(HEAD_DIM)


def attend(rows_of_head, keys_of_head, values_of_head, store):
    heads = range(LANE_HEADS)
    scores = [
        lax.dot_general(
            rows_of_head(h), keys_of_head(h), (((1,), (1,)), ((), ())), preferred_element_type=F32
        )
        for h in heads
    ]
    tops = [jnp.max(s, axis=1, keepdims=True) * SCALE for s in scores]
    weights = [jnp.exp2(s * SCALE - top).astype(BF16) for s, top in zip(scores, tops)]
    stats = 0.0
    for h in heads:
        both = jnp.dot(weights[h], values_of_head(h), preferred_element_type=F32)
        mixed, total = both[:, :HEAD_DIM], both[:, HEAD_DIM:]
        store(h, mixed / total)
        lane = lax.broadcasted_iota(jnp.int32, total.shape, 1)
        stats = jnp.where(lane == h, tops[h] + jnp.log2(total), stats)
    return stats


def join(part, part_lse, other, other_lse):
    top = jnp.maximum(part_lse, other_lse)
    a = jnp.exp2(part_lse - top)
    b = jnp.exp2(other_lse - top)
    total = a + b
    a = a / total
    b = b / total
    mixed = []
    for h in range(LANE_HEADS):
        cols = slice(h * HEAD_DIM, (h + 1) * HEAD_DIM)
        mixed.append(part[:, cols] * a[:, h : h + 1] + other[:, cols].astype(F32) * b[:, h : h + 1])
    return jnp.concatenate(mixed, axis=1), top + jnp.log2(total)


def kernel(
    q_ref, k_ref, v_ref, clip_ref, out_ref,
    qb, kb, vb, kl, vl, qa, stage, part, part_lse, hpart, hlse, extra, oin, oout, lin, lout, cw,
    load_sem, clip_sem, sib_send, sib_recv, left_send, left_recv,
    q_send, q_recv, o_send, o_recv, l_send, l_recv, out_sem, out_send, out_recv,
):
    size = lax.axis_size("ctx")
    chips = size // 2
    me = lax.axis_index("ctx")
    core = lax.rem(me, 2)
    chip = me // 2
    sib = chip * 2 + (1 - core)
    prev = lax.rem(me + size - 2, size)
    nxt = lax.rem(me + 2, size)
    prev_sib = prev + 1 - 2 * core
    nxt_sib = nxt + 1 - 2 * core

    def remote(src, dst, send, recv, to):
        return pltpu.make_async_remote_copy(
            src_ref=src, dst_ref=dst, send_sem=send, recv_sem=recv,
            device_id={"ctx": to}, device_id_type=MESH,
        )

    mine = pl.ds(pl.multiple_of(core * HALF, HALF), HALF)
    theirs = pl.ds(pl.multiple_of((1 - core) * HALF, HALF), HALF)
    whole = pl.ds(0, HALF)
    front = pl.ds(0, HEAD_DIM)

    def moves(base):
        pairs = [(q_ref.at[whole, pl.ds(pl.multiple_of(base, HALF), HALF)], qb.at[0, mine])]
        for src, dst in ((k_ref, kb), (v_ref, vb)):
            for h in range(LANE_HEADS):
                cols = pl.ds(pl.multiple_of(base + h * HEAD_DIM, HEAD_DIM), HEAD_DIM)
                pairs.append((src.at[whole, cols], dst.at[h, mine, front]))
        return pairs

    loads = [
        pltpu.make_async_copy(src, dst, load_sem.at[i])
        for i, (src, dst) in enumerate(moves(core * HALF))
    ]
    for copy in loads:
        copy.start()
    clips = []
    for i in range(HOPS + 2):
        row = pl.multiple_of(lax.rem(chip + chips - 1 + i, chips) * 8, 8)
        clips.append(
            pltpu.make_async_copy(clip_ref.at[pl.ds(row, 8)], cw.at[pl.ds(8 * i, 8)], clip_sem.at[i])
        )
    for copy in clips:
        copy.start()
    lin[...] = jnp.zeros(lin.shape, F32)

    barrier = pltpu.get_barrier_semaphore()
    for to in (sib, prev, nxt, prev_sib, nxt_sib):
        pl.semaphore_signal(barrier, inc=1, device_id={"ctx": to}, device_id_type=MESH)

    for copy in clips:
        copy.wait()
    lane = lax.broadcasted_iota(jnp.int32, (128, 128), 1)

    def clip_columns(row):
        wide = jnp.broadcast_to(cw[pl.ds(row, 1), :].astype(F32), (128, 128))
        return wide.T.astype(jnp.int32)

    ones = jnp.ones((128, HEAD_DIM), BF16)

    def prepare_own():
        @pl.loop(0, 8)
        def _(i):
            same = clip_columns(8 + i) == lane
            r = pl.ds(pl.multiple_of(i * 128, 128), 128)
            mask = jnp.where(same | (lane >= 32), 0.0, -PENALTY).astype(BF16)
            for h in range(LANE_HEADS):
                kb[h, r, HEAD_DIM:] = mask
                vb[h, r, HEAD_DIM:] = ones
            qa[0, r, :] = jnp.where(same, 1.0, 0.0).astype(BF16)

    def prepare_left():
        @pl.loop(0, 4)
        def _(i):
            same = clip_columns(4 + i) == lane
            r = pl.ds(pl.multiple_of(i * 128, 128), 128)
            mask = jnp.where(same | (lane >= 32), 0.0, -PENALTY).astype(BF16)
            for h in range(LANE_HEADS):
                kl[h, r, HEAD_DIM:] = mask
                vl[h, r, HEAD_DIM:] = ones

    def prepare_visitors(start):
        @pl.loop(0, 12)
        def _(i):
            i = start + i
            same = clip_columns(16 + i) == lane
            r = pl.ds(pl.multiple_of(lax.rem(i, 8) * 128, 128), 128)
            qa[1 + i // 8, r, :] = jnp.where(same, 1.0, 0.0).astype(BF16)

    prepare_own()
    prepare_visitors(0)
    prepare_visitors(12)
    prepare_left()
    pl.semaphore_wait(barrier, 5)

    swaps = [
        remote(src, dst, sib_send.at[i], sib_recv.at[i], sib)
        for i, (src, dst) in enumerate(moves((1 - core) * HALF))
    ]

    def rows_of(k):
        return pl.ds(pl.multiple_of(lax.rem(k + K // 2, K) * T, T), T)

    def send_q(d, k):
        r = rows_of(k)
        return remote(qb.at[d - 1, r], qb.at[d, r], q_send.at[d - 1], q_recv.at[d - 1, k], prev)

    def send_own(k, lane, to):
        rows = pl.ds(pl.multiple_of(lax.rem(k, K // 2) * T, T), T)
        cols = pl.ds(lane * WIDTH, WIDTH)
        return remote(q_ref.at[rows, cols], qb.at[1, rows_of(k)], q_send.at[0], q_recv.at[0, k], to)

    def start_own(k):
        @pl.when(core == 1 - k // (K // 2))
        def _():
            for lane in range(2):
                send_own(k, lane, 2 * (prev // 2) + lane).start()

    def send_o(d, k):
        r = rows_of(k)
        return remote(oout.at[d, r], oin.at[d - 1, r], o_send.at[d - 1], o_recv.at[d - 1, k], nxt)

    def send_l(d, k):
        rows = pl.ds(0, LANE_HEADS)
        return remote(
            lout.at[d, k, rows], lin.at[d - 1, k, rows], l_send.at[d - 1], l_recv.at[d - 1, k], nxt
        )

    def left_copy(lane, i):
        src, dst = ((k_ref, kl), (v_ref, vl))[i // LANE_HEADS]
        h = i % LANE_HEADS
        cols = pl.ds(lane * WIDTH + h * HEAD_DIM, HEAD_DIM)
        return remote(
            src.at[whole, cols], dst.at[h, :, front], left_send.at[lane, i], left_recv.at[i],
            2 * (nxt // 2) + lane,
        )

    start_own(0)

    @pl.when(core == 1)
    def _():
        for i in range(2 * LANE_HEADS):
            for lane in range(2):
                left_copy(lane, i).start()

    for copy in swaps:
        copy.start()

    stage[...] = jnp.zeros(stage.shape, BF16)
    blank = jnp.zeros((128 - T, 128), F32)

    def own_block(b):
        rows, seen = pl.ds(b * FRAME, FRAME), pl.ds(0, (b + 1) * FRAME)

        def queries(h):
            return jnp.concatenate(
                [qb[0, rows, h * HEAD_DIM : (h + 1) * HEAD_DIM], qa[0, rows, :]], axis=1
            )

        def store(h, value):
            hpart[rows, h * HEAD_DIM : (h + 1) * HEAD_DIM] = value

        hlse[rows, :] = attend(queries, lambda h: kb[h, seen, :], lambda h: vb[h, seen, :], store)

    def hand_on(d, k, mixed, lse):
        oout[d, rows_of(k), :] = mixed.astype(BF16)
        if d > 0:
            send_o(d, k).start()
            lout[d, k] = lse.T[:8, :]
            send_l(d, k).start()

    def piece_out(k):
        rows = pl.ds(pl.multiple_of(lax.rem(k, K // 2) * T, T), T)
        return oout.at[0, rows_of(k)], out_ref.at[rows, mine]

    def give_local(k):
        src, dst = piece_out(k)
        return pltpu.make_async_copy(src, dst, out_sem.at[lax.rem(k, K // 2)])

    def give_remote(k):
        src, dst = piece_out(k)
        i = lax.rem(k, K // 2)
        return remote(src, dst, out_send.at[i], out_recv.at[i], sib)

    @pl.loop(0, K + 2 * HOPS)
    def _(j):
        for d in range(HOPS, 0, -1):
            k = j - HOPS - (HOPS - d)
            here = slice((d - 1) * T, d * T)

            @pl.when((k >= 0) & (k < K))
            def _(d=d, k=k, here=here):
                if d == HOPS:
                    send_q(HOPS, k).wait_recv()
                r = rows_of(k)
                for h in range(LANE_HEADS):
                    stage[h, here, :HEAD_DIM] = qb[d, r, h * HEAD_DIM : (h + 1) * HEAD_DIM]
                    stage[h, here, HEAD_DIM:] = qa[d, r, :]

        @pl.when((j >= HOPS) & (j < K + 2 * HOPS - 1))
        def _():
            def store(h, value):
                part[:, h * HEAD_DIM : (h + 1) * HEAD_DIM] = value

            part_lse[...] = attend(
                lambda h: stage[h], lambda h: kb[h], lambda h: vb[h], store
            )

        far = slice((HOPS - 1) * T, HOPS * T)

        @pl.when((j >= HOPS + K // 2) & (j < HOPS + K))
        def _():
            @pl.when(j == HOPS + K // 2)
            def _():
                for i in range(2 * LANE_HEADS):
                    left_copy(0, i).wait_recv()

            def store(h, value):
                extra[:, h * HEAD_DIM : (h + 1) * HEAD_DIM] = value

            lse = attend(lambda h: stage[h, far, :], lambda h: kl[h], lambda h: vl[h], store)
            mixed, lse = join(part[far, :], part_lse[far, :], extra[...], lse)
            part[far, :] = mixed
            part_lse[far, :] = lse

        @pl.when((j >= HOPS) & (j < HOPS + K))
        def _():
            hand_on(HOPS, j - HOPS, part[far, :], part_lse[far, :])

        for hop in range(HOPS - 1, 0, -1):
            @pl.when((j >= hop) & (j < K + hop))
            def _(hop=hop):
                send_q(hop, j - hop).wait_recv()
                send_q(hop + 1, j - hop).start()

        @pl.when((j >= 1) & (j < K))
        def _():
            start_own(j)

        for b in range(CHIP // FRAME):
            @pl.when(j == b)
            def _(b=b):
                if b == 0:
                    for load, swap in zip(loads, swaps):
                        load.wait()
                        swap.wait_recv()
                own_block(b)

        for d in range(HOPS - 1, -1, -1):
            k = j - HOPS - (HOPS - d)

            @pl.when((k >= 0) & (k < K))
            def _(d=d, k=k):
                send_l(d + 1, k).wait_recv()
                send_o(d + 1, k).wait_recv()
                r = rows_of(k)
                arrived = jnp.concatenate([lin[d, k], jnp.zeros((120, 128), F32)], axis=0).T[:T, :]
                if d == 0:
                    mixed, lse = join(hpart[r, :], hlse[r, :], oin[d, r, :], arrived)
                else:
                    here = slice((d - 1) * T, d * T)
                    mixed, lse = join(part[here, :], part_lse[here, :], oin[d, r, :], arrived)
                hand_on(d, k, mixed, lse)
                if d == 0:
                    for owner in range(2):
                        @pl.when((k // (K // 2) == 1 - owner) & (core == owner))
                        def _():
                            give_local(k).start()

                        @pl.when((k // (K // 2) == 1 - owner) & (core != owner))
                        def _():
                            give_remote(k).start()

    for copy in swaps:
        copy.wait_send()

    @pl.when(core == 1)
    def _():
        for i in range(2 * LANE_HEADS):
            for lane in range(2):
                left_copy(lane, i).wait_send()

    for d in range(1, HOPS + 1):
        remote(qb.at[d - 1], qb.at[d], q_send.at[d - 1], q_recv.at[d - 1, 0], prev).wait_send()
        remote(oout.at[d], oin.at[d - 1], o_send.at[d - 1], o_recv.at[d - 1, 0], nxt).wait_send()
        rows = pl.ds(0, LANE_HEADS)
        remote(
            lout.at[d, :, rows], lin.at[d - 1, :, rows], l_send.at[d - 1], l_recv.at[d - 1, 0], nxt
        ).wait_send()

    @pl.loop(0, K // 2)
    def _(k):
        give_local(k).wait()
        give_remote(k).wait()


def per_device(queries, keys, values, clip_ids):
    tokens, width = queries.shape
    anywhere = pl.BlockSpec(memory_space=pl.ANY)
    dma = pltpu.SemaphoreType.DMA
    stacked = HOPS * T
    moved = 1 + 2 * LANE_HEADS
    return pl.pallas_call(
        kernel,
        out_shape=jax.ShapeDtypeStruct((tokens, width), BF16),
        in_specs=[anywhere] * 4,
        out_specs=anywhere,
        scratch_shapes=[
            pltpu.VMEM((HOPS + 1, CHIP, WIDTH), BF16),
            pltpu.VMEM((LANE_HEADS, CHIP, 2 * HEAD_DIM), BF16),
            pltpu.VMEM((LANE_HEADS, CHIP, 2 * HEAD_DIM), BF16),
            pltpu.VMEM((LANE_HEADS, HALF, 2 * HEAD_DIM), BF16),
            pltpu.VMEM((LANE_HEADS, HALF, 2 * HEAD_DIM), BF16),
            pltpu.VMEM((HOPS + 1, CHIP, 128), BF16),
            pltpu.VMEM((LANE_HEADS, stacked, 2 * HEAD_DIM), BF16),
            pltpu.VMEM((stacked, WIDTH), F32),
            pltpu.VMEM((stacked, 128), F32),
            pltpu.VMEM((CHIP, WIDTH), F32),
            pltpu.VMEM((CHIP, 128), F32),
            pltpu.VMEM((T, WIDTH), F32),
            pltpu.VMEM((HOPS, CHIP, WIDTH), BF16),
            pltpu.VMEM((HOPS + 1, CHIP, WIDTH), BF16),
            pltpu.VMEM((HOPS, K, 8, 128), F32),
            pltpu.VMEM((HOPS + 1, K, 8, 128), F32),
            pltpu.VMEM((8 * (HOPS + 2), 128), jnp.int32),
            dma((moved,)), dma((HOPS + 2,)), dma((moved,)), dma((moved,)),
            dma((2, moved - 1)), dma((moved - 1,)),
            dma((HOPS,)), dma((HOPS, K)), dma((HOPS,)), dma((HOPS, K)), dma((HOPS,)), dma((HOPS, K)),
            dma((K // 2,)), dma((K // 2,)), dma((K // 2,)),
        ],
        compiler_params=pltpu.CompilerParams(
            collective_id=0, has_side_effects=True, vmem_limit_bytes=62 << 20
        ),
        name="chain_attention",
    )(queries, keys, values, clip_ids.reshape(-1, 128))


def solution(mesh):
    placed = (P(("dp", "ctx"), None), P(("dp", "ctx"), None), P(("dp", "ctx"), None), P("dp"))
    return jax.shard_map(
        per_device, mesh=mesh, in_specs=placed, out_specs=P(("dp", "ctx"), None), check_vma=False
    )
```

time: 294 us -> 113 us (0.38)
  the two profiles are of different devices: /device:TPU:24 before, /device:TPU:1 now
where the time goes in v2:
time: 113 us
  Pallas kernels  110 us (97%)
  local copies, waits for them, and re-layouts  2.26 us (2%)
    pallas_call x1, Pallas kernels, per_device(): pl.pallas_call(kernel, out_shape=jax.ShapeDtypeStruct((tokens, width), BF...  110 us
    unnamed x1, local copies, waits for them, and re-layouts  2.26 us

profile of v2, /device:TPU:1, one launch (start us, length us, event | category | flops | bytes accessed | tf_op | source)
XLA Modules:
  0.0 112.6 jit_solution(18153235670366491577)
XLA Ops:
  0.0 110.3 %chain_attention.1 = bf16[512,1024]{1,0:T(8,128)(2,1)} custom-call(bf16[512,1024]{1,0:T(8,128)(2,1)} %q_ref.1, bf16[512,1024]{1,0:T(8,128)(2,1)} %k_ref.1, bf16[512,1024]{1,0:T(8,128)(2,1)} %v_ref.1, s32[256,128]{1,0:T(8,128)} %bitcast.1), custom_call_target="tpu_custom_call" | custom-call | tf_op jit(solution)/shard_map/chain_attention/pallas_call | solution.py:370
  110.3 2.3 %copy.6 = bf16[512,1024]{1,0:T(8,128)(2,1)} copy(bf16[512,1024]{1,0:T(8,128)(2,1)} %chain_attention.1) | data formatting | bytes 2097152

commit v3 on v2

--- a/solution.py
+++ b/solution.py
@@ -20,6 +20,7 @@
 WIDTH = LANE_HEADS * HEAD_DIM
 T = 128
 K = CHIP // T
+REST = T
 HOPS = 3
 PENALTY = 16384.0
 SCALE = math.log2(math.e) / math.sqrt(HEAD_DIM)
@@ -61,8 +62,8 @@
 
 def kernel(
     q_ref, k_ref, v_ref, clip_ref, out_ref,
-    qb, kb, vb, kl, vl, qa, stage, part, part_lse, hpart, hlse, extra, oin, oout, lin, lout, cw,
-    load_sem, clip_sem, sib_send, sib_recv, left_send, left_recv,
+    qb, kb, vb, kl, vl, qa, far, far_lse, part, part_lse, hpart, hlse, extra, oin, oout, lin, lout, cw,
+    load_sem, clip_sem, sib_send, sib_recv, left_send, left_recv, rest_send, rest_recv,
     q_send, q_recv, o_send, o_recv, l_send, l_recv, out_sem, out_send, out_recv,
 ):
     size = lax.axis_size("ctx")
@@ -166,16 +167,20 @@
     ]
 
     def rows_of(k):
-        return pl.ds(pl.multiple_of(lax.rem(k + K // 2, K) * T, T), T)
+        block = jnp.where(k < K // 2, k + K // 2, K - 1 - k)
+        return pl.ds(pl.multiple_of(block * T, T), T)
+
+    def device_rows(k):
+        block = jnp.where(k < K // 2, k, K - 1 - k)
+        return pl.ds(pl.multiple_of(block * T, T), T)
 
     def send_q(d, k):
         r = rows_of(k)
         return remote(qb.at[d - 1, r], qb.at[d, r], q_send.at[d - 1], q_recv.at[d - 1, k], prev)
 
     def send_own(k, lane, to):
-        rows = pl.ds(pl.multiple_of(lax.rem(k, K // 2) * T, T), T)
         cols = pl.ds(lane * WIDTH, WIDTH)
-        return remote(q_ref.at[rows, cols], qb.at[1, rows_of(k)], q_send.at[0], q_recv.at[0, k], to)
+        return remote(q_ref.at[device_rows(k), cols], qb.at[1, rows_of(k)], q_send.at[0], q_recv.at[0, k], to)
 
     def start_own(k):
         @pl.when(core == 1 - k // (K // 2))
@@ -193,41 +198,56 @@
             lout.at[d, k, rows], lin.at[d - 1, k, rows], l_send.at[d - 1], l_recv.at[d - 1, k], nxt
         )
 
-    def left_copy(lane, i):
-        src, dst = ((k_ref, kl), (v_ref, vl))[i // LANE_HEADS]
-        h = i % LANE_HEADS
-        cols = pl.ds(lane * WIDTH + h * HEAD_DIM, HEAD_DIM)
+    def left_copy(i, early):
+        h = i // 2
+        src, mem, dst = ((k_ref, kb, kl), (v_ref, vb, vl))[i % 2]
+        if early:
+            cols = pl.ds(pl.multiple_of(core * WIDTH + h * HEAD_DIM, HEAD_DIM), HEAD_DIM)
+            part_of = src.at[pl.ds(REST, HALF - REST), cols]
+        else:
+            part_of = mem.at[h, pl.ds(HALF + REST, HALF - REST), front]
         return remote(
-            src.at[whole, cols], dst.at[h, :, front], left_send.at[lane, i], left_recv.at[i],
-            2 * (nxt // 2) + lane,
+            part_of, dst.at[h, pl.ds(REST, HALF - REST), front], left_send.at[i], left_recv.at[i], nxt
+        )
+
+    def rest_copy(i):
+        h = i // 2
+        mem, dst = ((kb, kl), (vb, vl))[i % 2]
+        return remote(
+            mem.at[h, pl.ds(HALF, REST), front], dst.at[h, pl.ds(0, REST), front],
+            rest_send.at[i], rest_recv.at[i], nxt,
         )
 
     start_own(0)
+    start_own(1)
 
     @pl.when(core == 1)
     def _():
         for i in range(2 * LANE_HEADS):
-            for lane in range(2):
-                left_copy(lane, i).start()
+            left_copy(i, True).start()
 
     for copy in swaps:
         copy.start()
 
-    stage[...] = jnp.zeros(stage.shape, BF16)
-    blank = jnp.zeros((128 - T, 128), F32)
+    def wide_rows(d, rows, h):
+        return jnp.concatenate([qb[d, rows, h * HEAD_DIM : (h + 1) * HEAD_DIM], qa[d, rows, :]], axis=1)
 
     def own_block(b):
         rows, seen = pl.ds(b * FRAME, FRAME), pl.ds(0, (b + 1) * FRAME)
-
-        def queries(h):
-            return jnp.concatenate(
-                [qb[0, rows, h * HEAD_DIM : (h + 1) * HEAD_DIM], qa[0, rows, :]], axis=1
-            )
+        if b == 0:
+            for load, swap in zip(loads, swaps):
+                load.wait()
+                swap.wait_recv()
+
+            @pl.when(core == 0)
+            def _():
+                for i in range(2 * LANE_HEADS):
+                    left_copy(i, False).start()
 
         def store(h, value):
             hpart[rows, h * HEAD_DIM : (h + 1) * HEAD_DIM] = value
 
-        hlse[rows, :] = attend(queries, lambda h: kb[h, seen, :], lambda h: vb[h, seen, :], store)
+        hlse[rows, :] = attend(lambda h: wide_rows(0, rows, h), lambda h: kb[h, seen, :], lambda h: vb[h, seen, :], store)
 
     def hand_on(d, k, mixed, lse):
         oout[d, rows_of(k), :] = mixed.astype(BF16)
@@ -237,8 +257,7 @@
             send_l(d, k).start()
 
     def piece_out(k):
-        rows = pl.ds(pl.multiple_of(lax.rem(k, K // 2) * T, T), T)
-        return oout.at[0, rows_of(k)], out_ref.at[rows, mine]
+        return oout.at[0, rows_of(k)], out_ref.at[device_rows(k), mine]
 
     def give_local(k):
         src, dst = piece_out(k)
@@ -249,111 +268,142 @@
         i = lax.rem(k, K // 2)
         return remote(src, dst, out_send.at[i], out_recv.at[i], sib)
 
-    @pl.loop(0, K + 2 * HOPS)
-    def _(j):
-        for d in range(HOPS, 0, -1):
-            k = j - HOPS - (HOPS - d)
-            here = slice((d - 1) * T, d * T)
-
-            @pl.when((k >= 0) & (k < K))
-            def _(d=d, k=k, here=here):
-                if d == HOPS:
-                    send_q(HOPS, k).wait_recv()
-                r = rows_of(k)
-                for h in range(LANE_HEADS):
-                    stage[h, here, :HEAD_DIM] = qb[d, r, h * HEAD_DIM : (h + 1) * HEAD_DIM]
-                    stage[h, here, HEAD_DIM:] = qa[d, r, :]
-
-        @pl.when((j >= HOPS) & (j < K + 2 * HOPS - 1))
+    def relay(hop, k):
+        send_q(hop, k).wait_recv()
+        send_q(hop + 1, k).start()
+
+    def farthest(k):
+        r = rows_of(k)
+        send_q(HOPS, k).wait_recv()
+
+        def store(h, value):
+            far[:, h * HEAD_DIM : (h + 1) * HEAD_DIM] = value
+
+        far_lse[...] = attend(
+            lambda h: wide_rows(HOPS, r, h), lambda h: kb[h], lambda h: vb[h], store
+        )
+
+        @pl.when(k == K // 2)
         def _():
-            def store(h, value):
-                part[:, h * HEAD_DIM : (h + 1) * HEAD_DIM] = value
-
-            part_lse[...] = attend(
-                lambda h: stage[h], lambda h: kb[h], lambda h: vb[h], store
-            )
-
-        far = slice((HOPS - 1) * T, HOPS * T)
-
-        @pl.when((j >= HOPS + K // 2) & (j < HOPS + K))
+            for i in range(2 * LANE_HEADS):
+                left_copy(i, False).wait_recv()
+
+        @pl.when(k == K - 1)
         def _():
-            @pl.when(j == HOPS + K // 2)
-            def _():
-                for i in range(2 * LANE_HEADS):
-                    left_copy(0, i).wait_recv()
+            for i in range(2 * LANE_HEADS):
+                rest_copy(i).wait_recv()
+
+        def reach(start):
+            keys = pl.ds(start, HALF - start)
 
             def store(h, value):
                 extra[:, h * HEAD_DIM : (h + 1) * HEAD_DIM] = value
 
-            lse = attend(lambda h: stage[h, far, :], lambda h: kl[h], lambda h: vl[h], store)
-            mixed, lse = join(part[far, :], part_lse[far, :], extra[...], lse)
-            part[far, :] = mixed
-            part_lse[far, :] = lse
-
-        @pl.when((j >= HOPS) & (j < HOPS + K))
+            lse = attend(
+                lambda h: wide_rows(HOPS, r, h), lambda h: kl[h, keys, :], lambda h: vl[h, keys, :], store
+            )
+            mixed, lse = join(far[...], far_lse[...], extra[...], lse)
+            far[...] = mixed
+            far_lse[...] = lse
+
+        @pl.when((k >= K // 2) & (k < K - 1))
         def _():
-            hand_on(HOPS, j - HOPS, part[far, :], part_lse[far, :])
-
-        for hop in range(HOPS - 1, 0, -1):
-            @pl.when((j >= hop) & (j < K + hop))
-            def _(hop=hop):
-                send_q(hop, j - hop).wait_recv()
-                send_q(hop + 1, j - hop).start()
-
-        @pl.when((j >= 1) & (j < K))
+            reach(REST)
+
+        @pl.when(k == K - 1)
         def _():
-            start_own(j)
-
-        for b in range(CHIP // FRAME):
-            @pl.when(j == b)
-            def _(b=b):
-                if b == 0:
-                    for load, swap in zip(loads, swaps):
-                        load.wait()
-                        swap.wait_recv()
-                own_block(b)
-
-        for d in range(HOPS - 1, -1, -1):
-            k = j - HOPS - (HOPS - d)
-
-            @pl.when((k >= 0) & (k < K))
-            def _(d=d, k=k):
-                send_l(d + 1, k).wait_recv()
-                send_o(d + 1, k).wait_recv()
-                r = rows_of(k)
-                arrived = jnp.concatenate([lin[d, k], jnp.zeros((120, 128), F32)], axis=0).T[:T, :]
-                if d == 0:
-                    mixed, lse = join(hpart[r, :], hlse[r, :], oin[d, r, :], arrived)
-                else:
-                    here = slice((d - 1) * T, d * T)
-                    mixed, lse = join(part[here, :], part_lse[here, :], oin[d, r, :], arrived)
-                hand_on(d, k, mixed, lse)
-                if d == 0:
-                    for owner in range(2):
-                        @pl.when((k // (K // 2) == 1 - owner) & (core == owner))
-                        def _():
-                            give_local(k).start()
-
-                        @pl.when((k // (K // 2) == 1 - owner) & (core != owner))
-                        def _():
-                            give_remote(k).start()
-
-    for copy in swaps:
-        copy.wait_send()
-
-    @pl.when(core == 1)
-    def _():
+            reach(0)
+
+        hand_on(HOPS, k, far[...], far_lse[...])
+
+    def nearer(i, k):
+        r = rows_of(k)
+
+        def store(h, value):
+            part[i, :, h * HEAD_DIM : (h + 1) * HEAD_DIM] = value
+
+        part_lse[i] = attend(
+            lambda h: jnp.concatenate([wide_rows(d, r, h) for d in range(1, HOPS)], axis=0),
+            lambda h: kb[h], lambda h: vb[h], store,
+        )
+
+    def join_piece(d, i, k):
+        r = rows_of(k)
+        send_l(d + 1, k).wait_recv()
+        send_o(d + 1, k).wait_recv()
+        arrived = jnp.concatenate([lin[d, k], jnp.zeros((120, 128), F32)], axis=0).T[:T, :]
+        if d == 0:
+            mixed, lse = join(hpart[r, :], hlse[r, :], oin[d, r, :], arrived)
+        else:
+            here = slice((d - 1) * T, d * T)
+            mixed, lse = join(part[i, here, :], part_lse[i, here, :], oin[d, r, :], arrived)
+        hand_on(d, k, mixed, lse)
+        if d == 0:
+            for owner in range(2):
+                @pl.when((k // (K // 2) == 1 - owner) & (core == owner))
+                def _():
+                    give_local(k).start()
+
+                @pl.when((k // (K // 2) == 1 - owner) & (core != owner))
+                def _():
+                    give_remote(k).start()
+
+    def all_sent():
+        for copy in swaps:
+            copy.wait_send()
+
         for i in range(2 * LANE_HEADS):
-            for lane in range(2):
-                left_copy(lane, i).wait_send()
-
-    for d in range(1, HOPS + 1):
-        remote(qb.at[d - 1], qb.at[d], q_send.at[d - 1], q_recv.at[d - 1, 0], prev).wait_send()
-        remote(oout.at[d], oin.at[d - 1], o_send.at[d - 1], o_recv.at[d - 1, 0], nxt).wait_send()
-        rows = pl.ds(0, LANE_HEADS)
-        remote(
-            lout.at[d, :, rows], lin.at[d - 1, :, rows], l_send.at[d - 1], l_recv.at[d - 1, 0], nxt
-        ).wait_send()
+            left_copy(i, False).wait_send()
+            rest_copy(i).wait_send()
+
+        for d in range(1, HOPS + 1):
+            remote(qb.at[d - 1], qb.at[d], q_send.at[d - 1], q_recv.at[d - 1, 0], prev).wait_send()
+            remote(oout.at[d], oin.at[d - 1], o_send.at[d - 1], o_recv.at[d - 1, 0], nxt).wait_send()
+            rows = pl.ds(0, LANE_HEADS)
+            remote(
+                lout.at[d, :, rows], lin.at[d - 1, :, rows], l_send.at[d - 1], l_recv.at[d - 1, 0], nxt
+            ).wait_send()
+
+    @pl.loop(0, K // 2 + 2)
+    def _(p):
+        hopping = p < K // 2
+        coming = (p >= 1) & (p < K // 2 + 1)
+        home = p >= 2
+
+        def at(cond, *steps):
+            @pl.when(cond)
+            def _():
+                for step in steps:
+                    step()
+
+        k, before, last = 2 * p, 2 * (p - 1), 2 * (p - 2)
+        at(coming, lambda: farthest(before))
+        at(coming, lambda: farthest(before + 1))
+        at(hopping, lambda: relay(1, k))
+        at(p == 0, lambda: own_block(0))
+        at(coming, lambda: nearer(0, before), lambda: join_piece(2, 0, before))
+        at(p == 1, *[rest_copy(i).start for i in range(0, 1)])
+        at(p == 2, *[rest_copy(i).start for i in range(4, 5)])
+        at(hopping, lambda: relay(1, k + 1))
+        at(p == 0, lambda: own_block(1))
+        at(hopping, lambda: relay(2, k))
+        at(coming, lambda: nearer(1, before + 1), lambda: join_piece(2, 1, before + 1))
+        at(p == 1, *[rest_copy(i).start for i in range(1, 2)])
+        at(p == 2, *[rest_copy(i).start for i in range(5, 6)])
+        at(p == 0, lambda: own_block(2))
+        at(home, lambda: join_piece(0, 0, last))
+        at(p == K // 2 + 1, all_sent)
+        at(coming, lambda: join_piece(1, 0, before))
+        at(p == 1, *[rest_copy(i).start for i in range(2, 3)])
+        at(p == 2, *[rest_copy(i).start for i in range(6, 7)])
+        at(hopping, lambda: relay(2, k + 1))
+        at(p < K // 2 - 1, lambda: start_own(k + 2))
+        at(p < K // 2 - 1, lambda: start_own(k + 3))
+        at(p == 0, lambda: own_block(3))
+        at(home, lambda: join_piece(0, 1, last + 1))
+        at(coming, lambda: join_piece(1, 1, before + 1))
+        at(p == 1, *[rest_copy(i).start for i in range(3, 4)])
+        at(p == 2, *[rest_copy(i).start for i in range(7, 8)])
 
     @pl.loop(0, K // 2)
     def _(k):
@@ -361,13 +411,30 @@
         give_remote(k).wait()
 
 
+PLACES = 4
+
+
+def place(src, dst, held, sem_in, sem_out):
+    rows = src.shape[0] // PLACES
+    spans = [pl.ds(i * rows, rows) for i in range(PLACES)]
+    ins = [pltpu.make_async_copy(src.at[r], held.at[r], sem_in.at[i]) for i, r in enumerate(spans)]
+    outs = [pltpu.make_async_copy(held.at[r], dst.at[r], sem_out.at[i]) for i, r in enumerate(spans)]
+    for copy in ins:
+        copy.start()
+    for first, second in zip(ins, outs):
+        first.wait()
+        second.start()
+    for copy in outs:
+        copy.wait()
+
+
 def per_device(queries, keys, values, clip_ids):
     tokens, width = queries.shape
     anywhere = pl.BlockSpec(memory_space=pl.ANY)
     dma = pltpu.SemaphoreType.DMA
-    stacked = HOPS * T
+    stacked = (HOPS - 1) * T
     moved = 1 + 2 * LANE_HEADS
-    return pl.pallas_call(
+    joined = pl.pallas_call(
         kernel,
         out_shape=jax.ShapeDtypeStruct((tokens, width), BF16),
         in_specs=[anywhere] * 4,
@@ -379,9 +446,10 @@
             pltpu.VMEM((LANE_HEADS, HALF, 2 * HEAD_DIM), BF16),
             pltpu.VMEM((LANE_HEADS, HALF, 2 * HEAD_DIM), BF16),
             pltpu.VMEM((HOPS + 1, CHIP, 128), BF16),
-            pltpu.VMEM((LANE_HEADS, stacked, 2 * HEAD_DIM), BF16),
-            pltpu.VMEM((stacked, WIDTH), F32),
-            pltpu.VMEM((stacked, 128), F32),
+            pltpu.VMEM((T, WIDTH), F32),
+            pltpu.VMEM((T, 128), F32),
+            pltpu.VMEM((2, stacked, WIDTH), F32),
+            pltpu.VMEM((2, stacked, 128), F32),
             pltpu.VMEM((CHIP, WIDTH), F32),
             pltpu.VMEM((CHIP, 128), F32),
             pltpu.VMEM((T, WIDTH), F32),
@@ -391,7 +459,7 @@
             pltpu.VMEM((HOPS + 1, K, 8, 128), F32),
             pltpu.VMEM((8 * (HOPS + 2), 128), jnp.int32),
             dma((moved,)), dma((HOPS + 2,)), dma((moved,)), dma((moved,)),
-            dma((2, moved - 1)), dma((moved - 1,)),
+            dma((moved - 1,)), dma((moved - 1,)), dma((moved - 1,)), dma((moved - 1,)),
             dma((HOPS,)), dma((HOPS, K)), dma((HOPS,)), dma((HOPS, K)), dma((HOPS,)), dma((HOPS, K)),
             dma((K // 2,)), dma((K // 2,)), dma((K // 2,)),
         ],
@@ -400,6 +468,14 @@
         ),
         name="chain_attention",
     )(queries, keys, values, clip_ids.reshape(-1, 128))
+    return pl.pallas_call(
+        place,
+        out_shape=jax.ShapeDtypeStruct((tokens, width), BF16),
+        in_specs=[anywhere],
+        out_specs=anywhere,
+        scratch_shapes=[pltpu.VMEM((tokens, width), BF16), dma((PLACES,)), dma((PLACES,))],
+        name="place_result",
+    )(joined)
 
 
 def solution(mesh):

time: 113 us -> 113 us (level)
  Pallas kernels: 110 us -> 113 us
  local copies, waits for them, and re-layouts: 2.26 us -> 0 us
    unnamed x1 -> x0, local copies, waits for them, and re-layouts: 2.26 us -> none
    pallas_call x0 -> x1, Pallas kernels: none -> 1.98 us  [per_device(): pl.pallas_call(place, out_shape=jax.ShapeDtypeStruct((tokens, width), BF1...]
where the time goes in v3:
time: 113 us
  Pallas kernels  113 us (100%)
    pallas_call x1, Pallas kernels, per_device(): pl.pallas_call(kernel, out_shape=jax.ShapeDtypeStruct((tokens, width), BF...  111 us

profile of v3, /device:TPU:1, one launch (start us, length us, event | category | flops | bytes accessed | tf_op | source)
XLA Modules:
  0.0 112.8 jit_solution(9939129057742361783)
XLA Ops:
  0.0 110.8 %chain_attention.1.src = bf16[512,1024]{1,0:T(8,128)(2,1)} custom-call(bf16[512,1024]{1,0:T(8,128)(2,1)} %q_ref.1, bf16[512,1024]{1,0:T(8,128)(2,1)} %k_ref.1, bf16[512,1024]{1,0:T(8,128)(2,1)} %v_ref.1, s32[256,128]{1,0:T(8,128)} %bitcast.1), custom_call_target="tpu_custom_call" | custom-call | tf_op jit(solution)/shard_map/chain_attention/pallas_call | solution.py:437
  110.9 2.0 %place_result.1 = bf16[512,1024]{1,0:T(8,128)(2,1)} custom-call(bf16[512,1024]{1,0:T(8,128)(2,1)} %chain_attention.1.src), custom_call_target="tpu_custom_call" | custom-call | tf_op jit(solution)/shard_map/place_result/pallas_call | solution.py:471
